TPU v7x, 32 devices: a whole 2x2x4 slice. The times are simulated.
32 devices in a mesh: hi: 8 (over y, x, core), lo: 4 (over z).
Axes of the slice: x: 2, y: 2, z: 4, core: 2. Of those that a mesh axis runs over, the one named last changes fastest.
Arguments:
- design: float32 [16, 524288], P(None, ('hi', 'lo')), may hold values from -24 to 24
- signs: int32 [524288], P(('hi', 'lo')), may hold values from -1 to 1, as said below
- samples: int32 [1024], replicated, may hold values from 0 to 524287, as said below
Outputs:
- sampled: float32 [16, 1024], P(None, ('hi', 'lo'))
- gram: float32 [16, 16], replicated
Inputs may be any that keep to these rules, and one draw needn't show every extreme that they name: `signs`: each is +1 or -1. `samples`: non-decreasing; the first is 0 and the last is 524287; an index may repeat.
All inputs are finite; a program needn't handle non-finite values.
Results may differ from a plain program's by a relative error of at most 0.000073.
Values sent between devices are 32-bit elements; how exact they have to be, the bound alone decides.
A program may use at most 64 MiB of HBM per device.

v0:
```python
import math

import jax
import jax.numpy as jnp
from jax import lax
from jax.sharding import PartitionSpec as P


def parity_signs(left, right, bit_count):
    common = jnp.bitwise_and(left, right)
    parity = jnp.zeros(common.shape, jnp.int32)
    for bit_number in range(bit_count):
        parity = parity + jnp.bitwise_and(jnp.right_shift(common, bit_number), 1)
    return (1 - 2 * (parity % 2)).astype(jnp.float32)


def hadamard_table(count):
    positions = jnp.arange(count, dtype=jnp.int32)
    return parity_signs(positions[:, None], positions[None, :], count.bit_length() - 1)


def local_transform(flipped):
    columns, length = flipped.shape
    bit_count = length.bit_length() - 1
    low_size = 2 ** (bit_count // 2)
    high_size = length // low_size
    blocks_view = flipped.reshape(columns, high_size, low_size)
    section = jnp.einsum(
        "cpq,qr->cpr", blocks_view, hadamard_table(low_size), precision=lax.Precision.HIGHEST
    )
    section = jnp.einsum(
        "cpq,pk->ckq", section, hadamard_table(high_size), precision=lax.Precision.HIGHEST
    )
    return section.reshape(columns, length)


def reduce_rows(term):
    return lax.psum_scatter(term, ("hi", "lo"), scatter_dimension=1, tiled=True)


def on_device(design, signs, samples):
    upper = lax.axis_size("hi")
    lower = lax.axis_size("lo")
    devices = upper * lower
    columns, length = design.shape
    device = lax.axis_index("hi") * lower + lax.axis_index("lo")
    flipped = design * signs.astype(jnp.float32)[None, :]
    local = local_transform(flipped)
    count = samples.shape[0]
    length_bits = length.bit_length() - 1
    sample_block = jnp.right_shift(samples, length_bits)
    within = jnp.bitwise_and(samples, length - 1)
    spread = lax.all_to_all(
        lax.all_to_all(
            local.reshape(columns, 1, 1, length), "hi", split_axis=3, concat_axis=1, tiled=True
        ),
        "lo",
        split_axis=3,
        concat_axis=2,
        tiled=True,
    )
    mixed = jnp.einsum(
        "chlt,hk->cklt", spread, hadamard_table(upper), precision=lax.Precision.HIGHEST
    )
    mixed = jnp.einsum(
        "chlt,lk->chkt", mixed, hadamard_table(lower), precision=lax.Precision.HIGHEST
    )
    slice_len = length // devices
    flat = mixed.reshape(columns, devices * slice_len)
    owner = within // slice_len
    position = sample_block * slice_len + within % slice_len
    picked = jnp.take(flat, position, axis=1)
    term = jnp.where((owner == device)[None, :], picked, jnp.float32(0.0))
    summed = reduce_rows(term)
    sampled = summed * (1.0 / math.sqrt(length * devices))
    partial_gram = jnp.dot(sampled, sampled.T, precision=lax.Precision.HIGHEST)
    gram = lax.psum(partial_gram, ("hi", "lo")) / count
    return (sampled, gram)


def solution(mesh):
    placed = (P(None, ("hi", "lo")), P(("hi", "lo")), P())
    return jax.shard_map(
        on_device,
        mesh=mesh,
        in_specs=placed,
        out_specs=(P(None, ("hi", "lo")), P()),
        check_vma=False,
    )
```

profile of v0, /device:TPU:0, one launch (start us, length us, event | category | flops | bytes accessed | tf_op | source)
XLA Modules:
  0.0 400.0 jit_solution(4142923551556463260)
XLA Ops:
  7.2 0.8 convert_element_type.18
  8.0 1.3 multiply_bitcast_fusion
  9.3 0.2 copy.33
  9.5 1.0 fusion.6
  10.6 1.1 convolution_bitcast_fusion.2
  11.7 4.6 %copy.29 = f32[16,128,128]{0,2,1:T(8,128)} copy(f32[16,128,128]{2,1,0:T(8,128)S(1)} %convolution_bitcast_fusion.2) | data formatting | bytes 2097152 | tf_op jit(solution)/shard_map/reshape;reshape | solution.py:55
  16.3 0.5 broadcast.173
  16.8 74.5 %reduce = f32[16384,16]{1,0:T(8,128)} reduce(f32[16384,1,1,16]{3,2,1,0:T(1,128)} %bitcast.39, f32[]{:T(128)} %broadcast.173), dimensions={1,2}, to_apply=%bitcast.30.reduce_sub_computation | reduce | bytes 2097156
  91.3 7.1 %reshape.38 = f32[8,1,32768]{2,1,0:T(1,128)S(1)} reshape(f32[16384,16]{1,0:T(8,128)} %reduce) | data formatting | bytes 2097152
  98.4 20.3 %all_to_all.24 = f32[8,1,32768]{2,1,0:T(1,128)S(1)} all-to-all(f32[8,1,32768]{2,1,0:T(1,128)S(1)} %reshape.38), channel_id=1, replica_groups=mesh['hi'=8,'lo'=4] {'hi'}, dimensions={0} | all-to-all | bytes 2097152 | tf_op jit(solution)/shard_map/all_to_all | solution.py:54
  118.7 3.1 reduce.1
  121.9 20.6 %reshape.39 = f32[16384,1,1,16]{3,2,1,0:T(1,128)} reshape(f32[8,32768]{1,0:T(8,128)S(1)} %reduce.1) | data formatting | bytes 2097152
  142.5 10.7 %copy.37 = f32[16,8,1,2048]{0,1,2,3:T(8,128)} copy(f32[16,8,1,2048]{0,3,1,2:T(8,128)} %bitcast.41) | data formatting | bytes 2097152 | tf_op jit(solution)/shard_map/all_to_all | solution.py:54
  153.2 0.0 copy-start
  153.2 6.4 %reshape.40 = f32[4,1,65536]{2,1,0:T(1,128)} reshape(f32[2048,1,8,16]{3,2,1,0:T(8,128)} %bitcast.42) | data formatting | bytes 2097152
  159.6 4.9 %all-to-all-start.1 = ((f32[4,1,65536]{2,1,0:T(1,128)}), f32[4,1,65536]{2,1,0:T(1,128)S(1)}, u32[]{:S(2)}, u32[]{:S(2)}) async-start(f32[4,1,65536]{2,1,0:T(1,128)} %reshape.40), calls=%async_computation.1 | async-start | bytes 2097152 | tf_op jit(solution)/shard_map/all_to_all | solution.py:53
  164.5 0.0 reduce-scatter.2.cloned.1.call-start
  164.5 0.0 copy-done
  164.5 25.0 %all-to-all-done.1 = f32[4,1,65536]{2,1,0:T(1,128)S(1)} async-done(((f32[4,1,65536]{2,1,0:T(1,128)}), f32[4,1,65536]{2,1,0:T(1,128)S(1)}, u32[]{:S(2)}, u32[]{:S(2)}) %all-to-all-start.1) | async-done | bytes 1048608 | tf_op jit(solution)/shard_map/all_to_all | solution.py:53
  189.5 3.7 reduce.2
  193.2 6.1 %reshape.41 = f32[2048,1,8,16]{3,2,1,0:T(8,128)} reshape(f32[4,65536]{1,0:T(4,128)S(1)} %reduce.2) | data formatting | bytes 2097152
  199.4 5.6 %copy.21 = f32[16,8,4,512]{3,1,2,0:T(8,128)S(1)} copy(f32[16,8,4,512]{0,1,3,2:T(8,128)} %bitcast.40) | data formatting | bytes 2097152 | tf_op jit(solution)/shard_map/all_to_all | solution.py:53
  205.0 1.0 convolution_bitcast_fusion.1
  206.0 2.4 convolution_bitcast_fusion
  208.4 4.6 %copy.32 = f32[16,8,4,512]{0,3,2,1:T(8,128)} copy(f32[16,8,4,512]{3,2,1,0:T(4,128)S(1)} %convolution_bitcast_fusion) | data formatting | bytes 2097152 | tf_op jit(solution)/shard_map/reshape | solution.py:69
  213.0 6.2 %gather_fusion = f32[1024,16]{1,0:T(8,128)S(1)} fusion(f32[16,16384]{0,1:T(8,128)} %bitcast.43, s32[1024]{0:T(1024)S(1)} %broadcast_clamp_fusion), kind=kCustom, calls=%fused_computation | custom fusion | bytes 135168 | tf_op jit(solution)/shard_map/jit(_take)/gather | solution.py:72
  219.2 1.1 select_bitcast_fusion
  220.3 0.0 reduce-scatter.2.cloned.1.call-update
  220.4 132.5 %reduce-scatter.2.cloned.1.call-done = f32[16,32]{0,1:T(8,128)} async-done(((f32[16,1024]{0,1:T(8,128)}), f32[16,32]{0,1:T(8,128)}) %reduce-scatter.2.cloned.1.call-update) | async-done | bytes 2064 | tf_op jit(solution)/shard_map/reduce_scatter | solution.py:38
  352.9 1.0 fusion.71
  353.8 36.9 %psum.7 = f32[16,16]{1,0:T(8,128)S(1)} all-reduce(f32[16,16]{1,0:T(8,128)S(1)} %fusion.71), channel_id=1, replica_groups=mesh['hi'=8,'lo'=4] {'hi','lo'}, use_global_device_ids=true, to_apply=%region_1.2 | all-reduce | flops 256 | bytes 2048 | tf_op jit(solution)/shard_map/psum | solution.py:77
  390.8 0.6 broadcast_multiply_fusion.1
  391.4 0.7 broadcast_multiply_fusion
  392.1 0.7 copy.24
  (2 shorter events, 0.0 us)
Async XLA Ops:
  153.2 11.3 %copy-start = (s32[1024]{0:T(1024)S(1)}, s32[1024]{0:T(1024)}, u32[]{:S(2)}) copy-start(s32[1024]{0:T(1024)} %param.5) | copy-start | bytes 12292
  159.6 29.9 %all-to-all-start.1 = ((f32[4,1,65536]{2,1,0:T(1,128)}), f32[4,1,65536]{2,1,0:T(1,128)S(1)}, u32[]{:S(2)}, u32[]{:S(2)}) async-start(f32[4,1,65536]{2,1,0:T(1,128)} %reshape.40), calls=%async_computation.1 | async-start | bytes 2097152 | tf_op jit(solution)/shard_map/all_to_all | solution.py:53
  164.5 188.4 %reduce-scatter.2.cloned.1.call-start = ((), (), s32[]{:S(2)}) async-start(), calls=%async_computation.3 | async-start | bytes 540672 | tf_op jit(solution)/shard_map/reduce_scatter | solution.py:38
Sparse Core Ops, SparseCore 0:
  220.5 132.3 reduce-scatter.1
where the time goes:
time: 407 us; the launch traced here: 400 us
  waiting for transfers between devices  158 us (39%)
  other arithmetic  85.9 us (21%)
  local copies, waits for them, and re-layouts  73.4 us (18%)
  blocking collectives  57.3 us (14%)
  between operations  14.6 us (4%)
  matrix products  6.49 us (2%)
  starting transfers between devices  4.87 us (1%)
    reduce_scatter x1, waiting for transfers between devices, reduce_rows(): return lax.psum_scatter(term, ('hi', 'lo'), scatter_dimension=1, tiled=True)  133 us
    unnamed x2, other arithmetic  75.8 us
    unnamed x9, local copies, waits for them, and re-layouts  41.7 us
    psum x1, blocking collectives, on_device(): gram = lax.psum(partial_gram, ('hi', 'lo')) / count  36.9 us
    all_to_all x1, waiting for transfers between devices, on_device(): lax.all_to_all(lax.all_to_all(local.reshape(columns, 1, 1, length), 'hi',...  25 us
    all_to_all x1, blocking collectives, on_device(): lax.all_to_all(local.reshape(columns, 1, 1, length), 'hi', split_axis=3,...  20.3 us
    all_to_all x1, local copies, waits for them, and re-layouts, on_device(): lax.all_to_all(local.reshape(columns, 1, 1, length), 'hi', split_axis=3,...  10.7 us
  transfers between devices with their start and end apart: 2, of which 2 were waited for; matrix products, arithmetic and copies ran while one was open for 0% of the time, Pallas kernels for 0%

commit v1 on v0

v1 whole, which is shorter than its diff:
```python
import functools
import math

import jax
import jax.numpy as jnp
from jax import lax
from jax.experimental import pallas as pl
from jax.experimental.pallas import tpu as pltpu
from jax.sharding import PartitionSpec as P

LANES = 128
LOW_BITS = 8
LOADS = 4


def bit_sign(values, bit):
    return (1 - 2 * jnp.bitwise_and(jnp.right_shift(values, bit), 1)).astype(jnp.float32)


def parity_sign(values, bits):
    step = 1
    while step < bits:
        values = jnp.bitwise_xor(values, jnp.right_shift(values, step))
        step *= 2
    return bit_sign(values, 0)


def low_table(rows):
    width = rows.shape[1]
    octet = lax.broadcasted_iota(jnp.int32, (8, width), 0)
    table = parity_sign(jnp.bitwise_and(octet, jnp.broadcast_to(rows, (8, width))), 3)
    blocks = [table]
    for bit in range(3, LOW_BITS):
        sign = jnp.broadcast_to(bit_sign(rows, bit), (8, width))
        blocks = blocks + [block * sign for block in blocks]
    return jnp.concatenate(blocks, axis=0).astype(jnp.bfloat16)


def sketch_kernel(
    sizes,
    design_hbm,
    signs_hbm,
    samples_ref,
    sampled_ref,
    gram_ref,
    design,
    signs,
    split,
    term,
    landed,
    part,
    grams,
    load_sem,
    sign_sem,
    send_hi,
    recv_hi,
    send_lo,
    recv_lo,
    send_gram,
    recv_gram,
):
    upper, lower, group, length, count = sizes
    columns = design.shape[0]
    low = 2**LOW_BITS
    high = length // low
    high_bits = high.bit_length() - 1
    length_bits = length.bit_length() - 1
    device_bits = (upper * lower).bit_length() - 1
    my_hi = lax.axis_index("hi")
    my_lo = lax.axis_index("lo")
    device = my_hi * lower + my_lo

    sign_load = pltpu.make_async_copy(signs_hbm, signs, sign_sem)
    sign_load.start()
    piece = length // LOADS
    loads = []
    for number in range(LOADS):
        here = pl.ds(number * piece, piece)
        loads.append(
            pltpu.make_async_copy(design_hbm.at[:, here], design.at[:, here], load_sem.at[number])
        )
        loads[-1].start()

    barrier = pltpu.get_barrier_semaphore()
    for step in range(1, upper):
        peer = lax.rem(my_hi + step, upper)
        pl.semaphore_signal(
            barrier, inc=1, device_id=(peer, my_lo), device_id_type=pl.DeviceIdType.MESH
        )
    for step in range(1, lower):
        peer = lax.rem(my_lo + step, lower)
        pl.semaphore_signal(
            barrier, inc=1, device_id=(my_hi, peer), device_id_type=pl.DeviceIdType.MESH
        )

    sign_load.wait()
    for number in range(LOADS):
        loads[number].wait()
        for block in range(number * high // LOADS, (number + 1) * high // LOADS):
            for half in range(low // LANES):
                lane = block * (low // LANES) + half
                value = design[:, lane * LANES : (lane + 1) * LANES] * signs[
                    lane : lane + 1, :
                ].astype(jnp.float32)
                top = value.astype(jnp.bfloat16)
                rest = (value - top.astype(jnp.float32)).astype(jnp.bfloat16)
                rows = slice(block * columns, (block + 1) * columns)
                split[rows, half * LANES : (half + 1) * LANES] = top
                split[rows, low + half * LANES : low + (half + 1) * LANES] = rest

    tiles = group // LANES
    per_chunk = max(1, 2 // tiles)
    chunks = upper // per_chunk
    width = per_chunk * group

    def to_hi(step):
        peer = lax.rem(my_hi + step, upper)
        return pltpu.make_async_remote_copy(
            src_ref=term.at[step - 1],
            dst_ref=landed.at[step - 1],
            send_sem=send_hi.at[step - 1],
            recv_sem=recv_hi.at[step - 1],
            device_id=(peer, my_lo),
            device_id_type=pl.DeviceIdType.MESH,
        )

    def chunk_term(chunk):
        rows = []
        for unit in range(per_chunk):
            target = lax.rem(my_hi + chunk * per_chunk + unit + 1, upper)
            for tile in range(tiles):
                rows.append(samples_ref[pl.ds(target * tiles + tile, 1), :])
        rows = jnp.concatenate(rows, axis=1)
        table = low_table(rows)
        table = jnp.concatenate([table, table], axis=0)
        product = jnp.dot(split[...], table, preferred_element_type=jnp.float32)
        blocks = [product[p * columns : (p + 1) * columns] for p in range(high)]
        for bit in range(high_bits):
            sign = jnp.broadcast_to(bit_sign(rows, LOW_BITS + bit), (columns, width))
            blocks = [blocks[2 * i] + sign * blocks[2 * i + 1] for i in range(len(blocks) // 2)]
        owner = jnp.bitwise_and(jnp.right_shift(rows, length_bits), device)
        total = blocks[0] * parity_sign(owner, device_bits)
        for unit in range(per_chunk):
            term[chunk * per_chunk + unit] = total[:, unit * group : (unit + 1) * group]

    def send_chunk(chunk):
        for unit in range(per_chunk):
            step = chunk * per_chunk + unit + 1
            to_hi(step).start()

    if chunks <= 4:
        for chunk in range(chunks):
            chunk_term(chunk)
            if chunk == 0:
                pl.semaphore_wait(barrier, upper + lower - 2)
            for unit in range(per_chunk):
                step = chunk * per_chunk + unit + 1
                if step < upper:
                    to_hi(step).start()
    else:
        pl.semaphore_wait(barrier, upper + lower - 2)

        @pl.loop(0, chunks)
        def _(chunk):
            chunk_term(chunk)
            for unit in range(per_chunk):
                step = chunk * per_chunk + unit + 1

                @pl.when(step < upper)
                def _():
                    to_hi(step).start()

    total = term[upper - 1]
    for step in range(1, upper):
        to_hi(step).wait_recv()
        total = total + landed[step - 1]
    part[my_lo] = total

    def to_lo(step):
        peer = lax.rem(my_lo + step, lower)
        return pltpu.make_async_remote_copy(
            src_ref=part.at[my_lo],
            dst_ref=part.at[my_lo],
            send_sem=send_lo.at[step - 1],
            recv_sem=recv_lo.at[step - 1],
            device_id=(my_hi, peer),
            device_id_type=pl.DeviceIdType.MESH,
        )

    for step in range(1, lower):
        to_lo(step).start()
    for step in range(1, lower):
        to_lo(step).wait_recv()
    total = part[0]
    for source in range(1, lower):
        total = total + part[source]
    sampled = total * (1.0 / math.sqrt(length * upper * lower))
    sampled_ref[...] = sampled
    grams[my_hi] = lax.dot_general(
        sampled,
        sampled,
        (((1,), (1,)), ((), ())),
        precision=lax.Precision.HIGHEST,
        preferred_element_type=jnp.float32,
    )

    def to_gram(step):
        peer = lax.rem(my_hi + step, upper)
        return pltpu.make_async_remote_copy(
            src_ref=grams.at[my_hi],
            dst_ref=grams.at[my_hi],
            send_sem=send_gram.at[step - 1],
            recv_sem=recv_gram.at[step - 1],
            device_id=(peer, my_lo),
            device_id_type=pl.DeviceIdType.MESH,
        )

    for step in range(1, upper):
        to_gram(step).start()
    for step in range(1, upper):
        to_gram(step).wait_recv()
    gram = grams[0]
    for source in range(1, upper):
        gram = gram + grams[source]
    gram_ref[...] = gram * (1.0 / count)
    for step in range(1, upper):
        to_hi(step).wait_send()
        to_gram(step).wait_send()
    for step in range(1, lower):
        to_lo(step).wait_send()


def on_device(design, signs, samples):
    upper = lax.axis_size("hi")
    lower = lax.axis_size("lo")
    columns, length = design.shape
    count = samples.shape[0]
    group = count // upper
    low = 2**LOW_BITS
    high = length // low
    sampled, gram = pl.pallas_call(
        functools.partial(sketch_kernel, (upper, lower, group, length, count)),
        out_shape=(
            jax.ShapeDtypeStruct((columns, group), jnp.float32),
            jax.ShapeDtypeStruct((columns, columns), jnp.float32),
        ),
        in_specs=[
            pl.BlockSpec(memory_space=pl.ANY),
            pl.BlockSpec(memory_space=pl.ANY),
            pl.BlockSpec(memory_space=pltpu.VMEM),
        ],
        out_specs=(
            pl.BlockSpec(memory_space=pltpu.VMEM),
            pl.BlockSpec(memory_space=pltpu.VMEM),
        ),
        scratch_shapes=[
            pltpu.VMEM((columns, length), jnp.float32),
            pltpu.VMEM((length // LANES, LANES), jnp.int32),
            pltpu.VMEM((high * columns, 2 * low), jnp.bfloat16),
            pltpu.VMEM((upper, columns, group), jnp.float32),
            pltpu.VMEM((upper - 1, columns, group), jnp.float32),
            pltpu.VMEM((lower, columns, group), jnp.float32),
            pltpu.VMEM((upper, columns, columns), jnp.float32),
            pltpu.SemaphoreType.DMA((LOADS,)),
            pltpu.SemaphoreType.DMA,
            pltpu.SemaphoreType.DMA((upper - 1,)),
            pltpu.SemaphoreType.DMA((upper - 1,)),
            pltpu.SemaphoreType.DMA((lower - 1,)),
            pltpu.SemaphoreType.DMA((lower - 1,)),
            pltpu.SemaphoreType.DMA((upper - 1,)),
            pltpu.SemaphoreType.DMA((upper - 1,)),
        ],
        compiler_params=pltpu.CompilerParams(
            collective_id=0, has_side_effects=True, vmem_limit_bytes=32 * 2**20
        ),
    )(
        design,
        signs.reshape(length // LANES, LANES),
        samples.reshape(count // LANES, LANES),
    )
    own = group // lower
    sampled = lax.dynamic_slice_in_dim(sampled, lax.axis_index("lo") * own, own, axis=1)
    return sampled, gram


def solution(mesh):
    placed = (P(None, ("hi", "lo")), P(("hi", "lo")), P())
    return jax.shard_map(
        on_device,
        mesh=mesh,
        in_specs=placed,
        out_specs=(P(None, ("hi", "lo")), P()),
        check_vma=False,
    )
```

time: 407 us -> 22.4 us (0.06); the launches traced: 400 us -> 22.2 us
  waiting for transfers between devices: 158 us -> 0 us
  other arithmetic: 85.9 us -> 0 us
  local copies, waits for them, and re-layouts: 73.4 us -> 4.02 us
  blocking collectives: 57.3 us -> 0 us
  Pallas kernels: 0 us -> 17.5 us
  between operations: 14.6 us -> 0.65 us
  matrix products: 6.49 us -> 0 us
  starting transfers between devices: 4.87 us -> 0 us
    reduce_scatter x1 -> x0, waiting for transfers between devices: 133 us -> none  [reduce_rows(): return lax.psum_scatter(term, ('hi', 'lo'), scatter_dimension=1, tiled=True)]
    unnamed x2 -> x0, other arithmetic: 75.8 us -> none
    unnamed x9 -> x7, local copies, waits for them, and re-layouts: 41.7 us -> 3.34 us
    psum x1 -> x0, blocking collectives: 36.9 us -> none  [on_device(): gram = lax.psum(partial_gram, ('hi', 'lo')) / count]
    all_to_all x1 -> x0, waiting for transfers between devices: 25 us -> none  [on_device(): lax.all_to_all(lax.all_to_all(local.reshape(columns, 1, 1, length), 'hi',...]
    all_to_all x1 -> x0, blocking collectives: 20.3 us -> none  [on_device(): lax.all_to_all(local.reshape(columns, 1, 1, length), 'hi', split_axis=3,...]
    pallas_call x0 -> x1, Pallas kernels: none -> 17.5 us  [on_device(): pl.pallas_call(functools.partial(sketch_kernel, (upper, lower, group, len...]
    all_to_all x2 -> x0, local copies, waits for them, and re-layouts: 16.3 us -> none  [the longest x1 10.7 us: on_device(): lax.all_to_all(local.reshape(columns, 1, 1, length), 'hi', split_axis=3,...]
  transfers between devices with their start and end apart: 2 -> 0, of which waited for: 2 -> 0; matrix products, arithmetic and copies ran while one was open for 0% -> 0% of each run, Pallas kernels for 0% -> 0%
where the time goes in v1:
time: 22.4 us; the launch traced here: 22.2 us
  Pallas kernels  17.5 us (78%)
  local copies, waits for them, and re-layouts  4.02 us (18%)
  between operations  0.65 us (3%)
    pallas_call x1, Pallas kernels, on_device(): pl.pallas_call(functools.partial(sketch_kernel, (upper, lower, group, len...  17.5 us
    unnamed x7, local copies, waits for them, and re-layouts  3.34 us
    dynamic_slice x1, local copies, waits for them, and re-layouts, on_device(): lax.dynamic_slice_in_dim(sampled, lax.axis_index('lo') * own, own, axis=1)  0.68 us

profile of v1, /device:TPU:0, one launch (start us, length us, event | category | flops | bytes accessed | tf_op | source)
XLA Modules:
  0.0 22.2 jit_solution(4263199614387598498)
XLA Ops:
  0.6 0.0 copy-start.2
  0.6 0.7 %copy-done.2 = s32[1024]{0:T(1024)S(1)} copy-done((s32[1024]{0:T(1024)S(1)}, s32[1024]{0:T(1024)}, u32[]{:S(2)}) %copy-start.2) | copy-done | bytes 4120
  1.3 0.0 copy-start
  1.3 1.2 %copy-done = f32[16,16384]{1,0:T(8,128)S(1)} copy-done((f32[16,16384]{1,0:T(8,128)S(1)}, f32[16,16384]{1,0:T(8,128)}, u32[]{:S(2)}) %copy-start) | copy-done | bytes 1048600
  2.5 0.0 copy-start.1
  2.5 0.8 %copy-done.1 = s32[16384]{0:T(1024)S(1)} copy-done((s32[16384]{0:T(1024)S(1)}, s32[16384]{0:T(1024)}, u32[]{:S(2)}) %copy-start.1) | copy-done | bytes 65560
  3.4 17.5 %shard_map.50 = (f32[16,128]{1,0:T(8,128)S(1)}, f32[16,16]{1,0:T(8,128)S(1)}) custom-call(f32[16,16384]{1,0:T(8,128)S(1)} %copy-done, s32[128,128]{1,0:T(8,128)S(1)} %bitcast.2, s32[8,128]{1,0:T(8,128)S(1)} %bitcast.3), custom_call_target="tpu_custom_call" | custom-call | tf_op jit(solution)/shard_map/pallas_call | solution.py:241
  20.9 0.7 %constant_dynamic-slice_fusion = f32[16,32]{1,0:T(8,128)} fusion(f32[16,128]{1,0:T(8,128)S(1)} %get-tuple-element.4, s32[]{:T(128)S(6)} %select_n.3), kind=kLoop, calls=%fused_computation | loop fusion | bytes 4100 | tf_op jit(solution)/shard_map/dynamic_slice | solution.py:282
  21.6 0.6 %copy.6 = f32[16,16]{1,0:T(8,128)} copy(f32[16,16]{1,0:T(8,128)S(1)} %get-tuple-element.9) | data formatting | bytes 2048
Async XLA Ops:
  0.6 0.7 %copy-start.2 = (s32[1024]{0:T(1024)S(1)}, s32[1024]{0:T(1024)}, u32[]{:S(2)}) copy-start(s32[1024]{0:T(1024)} %param.5) | copy-start | bytes 12292
  1.3 1.2 %copy-start = (f32[16,16384]{1,0:T(8,128)S(1)}, f32[16,16384]{1,0:T(8,128)}, u32[]{:S(2)}) copy-start(f32[16,16384]{1,0:T(8,128)} %design_hbm.1) | copy-start | bytes 3145732
  2.5 0.8 %copy-start.1 = (s32[16384]{0:T(1024)S(1)}, s32[16384]{0:T(1024)}, u32[]{:S(2)}) copy-start(s32[16384]{0:T(1024)} %param.4) | copy-start | bytes 196612

commit v2 on v1

v2 whole, which is shorter than its diff:
```python
import functools
import math

import jax
import jax.numpy as jnp
from jax import lax
from jax.experimental import pallas as pl
from jax.experimental.pallas import tpu as pltpu
from jax.sharding import PartitionSpec as P

LANES = 128
LOW_BITS = 8
LOADS = 4


def bit_sign(values, bit):
    return (1 - 2 * jnp.bitwise_and(jnp.right_shift(values, bit), 1)).astype(jnp.float32)


def parity_sign(values, bits):
    step = 1
    while step < bits:
        values = jnp.bitwise_xor(values, jnp.right_shift(values, step))
        step *= 2
    return bit_sign(values, 0)


def low_table(rows):
    width = rows.shape[1]
    octet = lax.broadcasted_iota(jnp.int32, (8, width), 0)
    table = parity_sign(jnp.bitwise_and(octet, jnp.broadcast_to(rows, (8, width))), 3)
    blocks = [table]
    for bit in range(3, LOW_BITS):
        sign = jnp.broadcast_to(bit_sign(rows, bit), (8, width))
        blocks = blocks + [block * sign for block in blocks]
    return jnp.concatenate(blocks, axis=0).astype(jnp.bfloat16)


def flip(index, mask, size):
    result = 0
    bit = 1
    while bit < size:
        result = result + bit * lax.rem(lax.div(index, bit) + lax.div(mask, bit), 2)
        bit *= 2
    return result


def sketch_kernel(
    sizes,
    design_hbm,
    signs_hbm,
    samples_hbm,
    packed_ref,
    design,
    signs,
    samples_ref,
    split,
    tables,
    term,
    landed,
    part,
    grams,
    load_sem,
    sign_sem,
    sample_sem,
    send_hi,
    recv_hi,
    send_lo,
    recv_lo,
    send_gram,
    recv_gram,
):
    upper, lower, group, length, count = sizes
    columns = design.shape[0]
    low = 2**LOW_BITS
    high = length // low
    high_bits = high.bit_length() - 1
    length_bits = length.bit_length() - 1
    device_bits = (upper * lower).bit_length() - 1
    my_hi = lax.axis_index("hi")
    my_lo = lax.axis_index("lo")
    device = my_hi * lower + my_lo

    sample_load = pltpu.make_async_copy(samples_hbm, samples_ref, sample_sem)
    sample_load.start()
    sign_load = pltpu.make_async_copy(signs_hbm, signs, sign_sem)
    sign_load.start()
    piece = length // LOADS
    loads = []
    for number in range(LOADS):
        here = pl.ds(number * piece, piece)
        loads.append(
            pltpu.make_async_copy(design_hbm.at[:, here], design.at[:, here], load_sem.at[number])
        )
        loads[-1].start()

    barrier = pltpu.get_barrier_semaphore()
    for step in range(upper - 1, 0, -1):
        peer = flip(my_hi, step, upper)
        pl.semaphore_signal(
            barrier, inc=1, device_id=(peer, my_lo), device_id_type=pl.DeviceIdType.MESH
        )
    for step in range(lower - 1, 0, -1):
        peer = flip(my_lo, step, lower)
        pl.semaphore_signal(
            barrier, inc=1, device_id=(my_hi, peer), device_id_type=pl.DeviceIdType.MESH
        )

    tiles = group // LANES
    per_chunk = max(1, 2 // tiles)
    chunks = upper // per_chunk
    width = per_chunk * group

    def masks_of(chunk):
        return [upper - 1 - chunk * per_chunk - unit for unit in range(per_chunk)]

    def chunk_rows(chunk):
        rows = []
        for mask in masks_of(chunk):
            target = flip(my_hi, mask, upper)
            for tile in range(tiles):
                rows.append(samples_ref[pl.ds(target * tiles + tile, 1), :])
        return jnp.concatenate(rows, axis=1)

    def to_hi(mask):
        return pltpu.make_async_remote_copy(
            src_ref=term.at[mask],
            dst_ref=landed.at[mask - 1],
            send_sem=send_hi.at[mask - 1],
            recv_sem=recv_hi.at[mask - 1],
            device_id=(flip(my_hi, mask, upper), my_lo),
            device_id_type=pl.DeviceIdType.MESH,
        )

    def chunk_term(chunk, rows, table):
        table = jnp.concatenate([table, table], axis=0)
        product = jnp.dot(split[...], table, preferred_element_type=jnp.float32)
        blocks = [product[p * columns : (p + 1) * columns] for p in range(high)]
        for bit in range(high_bits):
            sign = jnp.broadcast_to(bit_sign(rows, LOW_BITS + bit), (columns, width))
            blocks = [blocks[2 * i] + sign * blocks[2 * i + 1] for i in range(len(blocks) // 2)]
        owner = jnp.bitwise_and(jnp.right_shift(rows, length_bits), device)
        total = blocks[0] * parity_sign(owner, device_bits)
        for unit, mask in enumerate(masks_of(chunk)):
            term[mask] = total[:, unit * group : (unit + 1) * group]

    unrolled = chunks <= 4
    sample_load.wait()
    if unrolled:
        chunk_samples = [chunk_rows(chunk) for chunk in range(chunks)]
        for chunk in range(chunks):
            tables[chunk] = low_table(chunk_samples[chunk])

    sign_load.wait()
    for number in range(LOADS):
        loads[number].wait()
        for block in range(number * high // LOADS, (number + 1) * high // LOADS):
            for half in range(low // LANES):
                lane = block * (low // LANES) + half
                value = design[:, lane * LANES : (lane + 1) * LANES] * signs[
                    lane : lane + 1, :
                ].astype(jnp.float32)
                top = value.astype(jnp.bfloat16)
                rest = (value - top.astype(jnp.float32)).astype(jnp.bfloat16)
                rows = slice(block * columns, (block + 1) * columns)
                split[rows, half * LANES : (half + 1) * LANES] = top
                split[rows, low + half * LANES : low + (half + 1) * LANES] = rest

    if unrolled:
        for chunk in range(chunks):
            chunk_term(chunk, chunk_samples[chunk], tables[chunk])
            if chunk == 0:
                pl.semaphore_wait(barrier, upper + lower - 2)
            for mask in masks_of(chunk):
                if mask > 0:
                    to_hi(mask).start()
    else:
        pl.semaphore_wait(barrier, upper + lower - 2)

        @pl.loop(0, chunks)
        def _(chunk):
            rows = chunk_rows(chunk)
            chunk_term(chunk, rows, low_table(rows))
            for mask in masks_of(chunk):

                @pl.when(mask > 0)
                def _():
                    to_hi(mask).start()

    for mask in range(upper - 1, 0, -1):
        to_hi(mask).wait_recv()
    total = term[0]
    for mask in range(1, upper):
        total = total + landed[mask - 1]
    part[my_lo] = total

    def to_lo(step):
        peer = flip(my_lo, step, lower)
        return pltpu.make_async_remote_copy(
            src_ref=part.at[my_lo],
            dst_ref=part.at[my_lo],
            send_sem=send_lo.at[step - 1],
            recv_sem=recv_lo.at[step - 1],
            device_id=(my_hi, peer),
            device_id_type=pl.DeviceIdType.MESH,
        )

    for step in range(lower - 1, 0, -1):
        to_lo(step).start()
    for step in range(1, lower):
        to_lo(step).wait_recv()
    total = part[0]
    for source in range(1, lower):
        total = total + part[source]
    sampled = total * (1.0 / math.sqrt(length * upper * lower))
    grams[my_hi] = lax.dot_general(
        sampled,
        sampled,
        (((1,), (1,)), ((), ())),
        precision=lax.Precision.HIGHEST,
        preferred_element_type=jnp.float32,
    )

    def to_gram(step):
        peer = flip(my_hi, step, upper)
        return pltpu.make_async_remote_copy(
            src_ref=grams.at[my_hi],
            dst_ref=grams.at[my_hi],
            send_sem=send_gram.at[step - 1],
            recv_sem=recv_gram.at[step - 1],
            device_id=(peer, my_lo),
            device_id_type=pl.DeviceIdType.MESH,
        )

    for step in range(upper - 1, 0, -1):
        to_gram(step).start()
    own = group // lower
    piece = sampled[:, :own]
    for slot in range(1, lower):
        piece = jnp.where(my_lo == slot, sampled[:, slot * own : (slot + 1) * own], piece)
    for step in range(1, upper):
        to_gram(step).wait_recv()
    gram = grams[0]
    for source in range(1, upper):
        gram = gram + grams[source]
    packed_ref[...] = jnp.concatenate(
        [piece, gram * (1.0 / count), jnp.zeros((columns, LANES - own - columns), jnp.float32)],
        axis=1,
    )
    for step in range(1, upper):
        to_hi(step).wait_send()
        to_gram(step).wait_send()
    for step in range(1, lower):
        to_lo(step).wait_send()


def split_kernel(packed_ref, sampled_ref, gram_ref):
    own = sampled_ref.shape[1]
    sampled_ref[...] = packed_ref[:, :own]
    gram_ref[...] = packed_ref[:, own : own + gram_ref.shape[1]]


def on_device(design, signs, samples):
    upper = lax.axis_size("hi")
    lower = lax.axis_size("lo")
    columns, length = design.shape
    count = samples.shape[0]
    group = count // upper
    low = 2**LOW_BITS
    high = length // low
    packed = pl.pallas_call(
        functools.partial(sketch_kernel, (upper, lower, group, length, count)),
        out_shape=jax.ShapeDtypeStruct((columns, LANES), jnp.float32),
        in_specs=[
            pl.BlockSpec(memory_space=pltpu.HBM),
            pl.BlockSpec(memory_space=pltpu.HBM),
            pl.BlockSpec(memory_space=pltpu.HBM),
        ],
        out_specs=pl.BlockSpec(memory_space=pltpu.VMEM),
        scratch_shapes=[
            pltpu.VMEM((columns, length), jnp.float32),
            pltpu.VMEM((length // LANES, LANES), jnp.int32),
            pltpu.VMEM((count // LANES, LANES), jnp.int32),
            pltpu.VMEM((high * columns, 2 * low), jnp.bfloat16),
            pltpu.VMEM((4, low, max(group, 2 * LANES)), jnp.bfloat16),
            pltpu.VMEM((upper, columns, group), jnp.float32),
            pltpu.VMEM((upper - 1, columns, group), jnp.float32),
            pltpu.VMEM((lower, columns, group), jnp.float32),
            pltpu.VMEM((upper, columns, columns), jnp.float32),
            pltpu.SemaphoreType.DMA((LOADS,)),
            pltpu.SemaphoreType.DMA,
            pltpu.SemaphoreType.DMA,
            pltpu.SemaphoreType.DMA((upper - 1,)),
            pltpu.SemaphoreType.DMA((upper - 1,)),
            pltpu.SemaphoreType.DMA((lower - 1,)),
            pltpu.SemaphoreType.DMA((lower - 1,)),
            pltpu.SemaphoreType.DMA((upper - 1,)),
            pltpu.SemaphoreType.DMA((upper - 1,)),
        ],
        compiler_params=pltpu.CompilerParams(
            collective_id=0, has_side_effects=True, vmem_limit_bytes=60 * 2**20
        ),
    )(
        design,
        signs.reshape(length // LANES, LANES),
        samples.reshape(count // LANES, LANES),
    )
    own = group // lower
    return pl.pallas_call(
        split_kernel,
        out_shape=(
            jax.ShapeDtypeStruct((columns, own), jnp.float32),
            jax.ShapeDtypeStruct((columns, columns), jnp.float32),
        ),
        in_specs=[pl.BlockSpec(memory_space=pltpu.VMEM)],
        out_specs=(
            pl.BlockSpec(memory_space=pltpu.VMEM),
            pl.BlockSpec(memory_space=pltpu.VMEM),
        ),
    )(packed)


def solution(mesh):
    placed = (P(None, ("hi", "lo")), P(("hi", "lo")), P())
    return jax.shard_map(
        on_device,
        mesh=mesh,
        in_specs=placed,
        out_specs=(P(None, ("hi", "lo")), P()),
        check_vma=False,
    )
```

time: 22.4 us -> 20.1 us (0.90)
  local copies, waits for them, and re-layouts: 4.02 us -> 0 us
  Pallas kernels: 17.5 us -> 19.2 us
    unnamed x7 -> x0, local copies, waits for them, and re-layouts: 3.34 us -> none
    pallas_call x0 -> x1, Pallas kernels: none -> 1.37 us  [on_device(): pl.pallas_call(split_kernel, out_shape=(jax.ShapeDtypeStruct((columns, ow...]
    dynamic_slice x1 -> x0, local copies, waits for them, and re-layouts: 0.68 us -> none  [on_device(): lax.dynamic_slice_in_dim(sampled, lax.axis_index('lo') * own, own, axis=1)]
    pallas_call x1, Pallas kernels: 17.5 us -> 17.8 us  [on_device(): pl.pallas_call(functools.partial(sketch_kernel, (upper, lower, group, len...]
where the time goes in v2:
time: 20.1 us; the launch traced here: 19.9 us
  Pallas kernels  19.2 us (96%)
  between operations  0.64 us (3%)
    pallas_call x1, Pallas kernels, on_device(): pl.pallas_call(functools.partial(sketch_kernel, (upper, lower, group, len...  17.8 us
    pallas_call x1, Pallas kernels, on_device(): pl.pallas_call(split_kernel, out_shape=(jax.ShapeDtypeStruct((columns, ow...  1.37 us

profile of v2, /device:TPU:0, one launch (start us, length us, event | category | flops | bytes accessed | tf_op | source)
XLA Modules:
  0.0 19.9 jit_solution(12860949612994671093)
XLA Ops:
  0.6 17.8 %shard_map.50.packed_ref = f32[16,128]{1,0:T(8,128)} custom-call(f32[16,16384]{1,0:T(8,128)} %design_hbm.1, s32[128,128]{1,0:T(8,128)} %bitcast.2, s32[8,128]{1,0:T(8,128)} %bitcast.3), custom_call_target="tpu_custom_call" | custom-call | tf_op jit(solution)/shard_map/pallas_call | solution.py:271
  18.5 1.4 %shard_map.51 = (f32[16,32]{1,0:T(8,128)}, f32[16,16]{1,0:T(8,128)}) custom-call(f32[16,128]{1,0:T(8,128)} %shard_map.50.packed_ref), custom_call_target="tpu_custom_call" | custom-call | tf_op jit(solution)/shard_map/pallas_call | solution.py:309

commit v3 on v2

--- a/solution.py
+++ b/solution.py
@@ -9,8 +9,8 @@
 from jax.sharding import PartitionSpec as P
 
 LANES = 128
-LOW_BITS = 8
-LOADS = 4
+LOW_BITS = 7
+LOADS = 2
 
 
 def bit_sign(values, bit):
@@ -213,12 +213,15 @@
     for source in range(1, lower):
         total = total + part[source]
     sampled = total * (1.0 / math.sqrt(length * upper * lower))
-    grams[my_hi] = lax.dot_general(
+    gram = lax.dot_general(
         sampled,
         sampled,
         (((1,), (1,)), ((), ())),
         precision=lax.Precision.HIGHEST,
         preferred_element_type=jnp.float32,
+    )
+    grams[my_hi] = jnp.concatenate(
+        [gram, jnp.zeros((columns, LANES - columns), jnp.float32)], axis=1
     )
 
     def to_gram(step):
@@ -244,7 +247,7 @@
     for source in range(1, upper):
         gram = gram + grams[source]
     packed_ref[...] = jnp.concatenate(
-        [piece, gram * (1.0 / count), jnp.zeros((columns, LANES - own - columns), jnp.float32)],
+        [piece, gram[:, :columns] * (1.0 / count), jnp.zeros((columns, LANES - own - columns), jnp.float32)],
         axis=1,
     )
     for step in range(1, upper):
@@ -286,7 +289,7 @@
             pltpu.VMEM((upper, columns, group), jnp.float32),
             pltpu.VMEM((upper - 1, columns, group), jnp.float32),
             pltpu.VMEM((lower, columns, group), jnp.float32),
-            pltpu.VMEM((upper, columns, columns), jnp.float32),
+            pltpu.VMEM((upper, columns, LANES), jnp.float32),
             pltpu.SemaphoreType.DMA((LOADS,)),
             pltpu.SemaphoreType.DMA,
             pltpu.SemaphoreType.DMA,

time: 20.1 us -> 19.8 us (0.985)
  Pallas kernels: 19.2 us -> 18.9 us
    pallas_call x1, Pallas kernels: 17.8 us -> 17.6 us  [on_device(): pl.pallas_call(functools.partial(sketch_kernel, (upper, lower, group, len...]
where the time goes in v3:
time: 19.8 us; the launch traced here: 19.6 us
  Pallas kernels  18.9 us (95%)
  between operations  0.64 us (3%)
    pallas_call x1, Pallas kernels, on_device(): pl.pallas_call(functools.partial(sketch_kernel, (upper, lower, group, len...  17.6 us
    pallas_call x1, Pallas kernels, on_device(): pl.pallas_call(split_kernel, out_shape=(jax.ShapeDtypeStruct((columns, ow...  1.37 us

profile of v3, /device:TPU:0, one launch (start us, length us, event | category | flops | bytes accessed | tf_op | source)
XLA Modules:
  0.0 19.6 jit_solution(1234363305117740820)
XLA Ops:
  0.6 17.6 %shard_map.50.packed_ref = f32[16,128]{1,0:T(8,128)} custom-call(f32[16,16384]{1,0:T(8,128)} %design_hbm.1, s32[128,128]{1,0:T(8,128)} %bitcast.2, s32[8,128]{1,0:T(8,128)} %bitcast.3), custom_call_target="tpu_custom_call" | custom-call | tf_op jit(solution)/shard_map/pallas_call | solution.py:274
  18.2 1.4 %shard_map.51 = (f32[16,32]{1,0:T(8,128)}, f32[16,16]{1,0:T(8,128)}) custom-call(f32[16,128]{1,0:T(8,128)} %shard_map.50.packed_ref), custom_call_target="tpu_custom_call" | custom-call | tf_op jit(solution)/shard_map/pallas_call | solution.py:312
